TPU v7x, 1024 devices: a whole 8x8x8 slice. The times are simulated.
1024 devices in a mesh: dp: 2 (over core), expert: 64 (over y, x), tensor: 8 (over z).
Axes of the slice: x: 8, y: 8, z: 8, core: 2. Of those that a mesh axis runs over, the one named last changes fastest.
Arguments:
- latent: bfloat16 [16384, 1024], P(('dp', 'expert')), may hold values from -6 to 6
- grad_out: bfloat16 [16384, 1024], P(('dp', 'expert')), may hold values from -6 to 6
- expert_weights: bfloat16 [2, 128, 1024, 2048], P(None, 'expert', None, 'tensor'), may hold values from -0.1875 to 0.1875
- expert_ids: int32 [16384, 8], P(('dp', 'expert')), may hold values from 0 to 127, as said below
- slot_index: int32 [16384, 8], P(('dp', 'expert')), may hold values from 0 to 7, as said below
- kept: int32 [16384, 8], P(('dp', 'expert')), may hold values from 0 to 1
- gate_weights: float32 [16384, 8], P(('dp', 'expert')), may hold values from 0.1 to 1
Outputs:
- mixed: bfloat16 [16384, 1024], P(('dp', 'expert'), 'tensor')
- latent_grad: bfloat16 [16384, 1024], P(('dp', 'expert'), 'tensor')
- weight_grads: float32 [2, 128, 1024, 2048], P(None, 'expert', 'dp', 'tensor')
Inputs may be any that keep to these rules, and one draw needn't show every extreme that they name: `expert_ids`: each token names 8 different experts. `slot_index`: kept pairs of one block of 128 tokens and one expert have distinct slots; slot 7 is used in every block, and one expert has all its 8 slots used in every block of one dp index.
All inputs are finite; a program needn't handle non-finite values.
Results may differ from a plain program's by a relative error of at most 0.02.
Values may be sent and summed in bfloat16 or wider, within the bound.
A program may use at most 64 MiB of HBM per device.

v0:
```python
import jax
import jax.numpy as jnp
from jax import lax
from jax.sharding import PartitionSpec as P


def shards(latent, grad_out, expert_weights, expert_ids, slot_index, kept, gate_weights):
    ntok, topk = expert_ids.shape
    owners = lax.axis_size("expert")
    local = expert_weights.shape[1]
    experts = owners * local
    cap = ntok * topk // experts
    width = latent.shape[1]
    quarter = width // lax.axis_size("tensor")
    dump = experts * cap
    target = jnp.where(kept > 0, expert_ids * cap + slot_index, dump)
    pairs = jnp.arange(ntok * topk, dtype=jnp.int32)
    source = jnp.full((dump + 1,), ntok * topk, jnp.int32).at[target.reshape(-1)].set(pairs)[:dump]
    token_of = source // topk
    zero_row = jnp.zeros((1, width), jnp.bfloat16)
    lat_pad = jnp.concatenate([latent, zero_row], 0)
    grad_pad = jnp.concatenate([grad_out, zero_row], 0)
    gate_pad = jnp.concatenate([gate_weights.reshape(-1), jnp.zeros((1,), jnp.float32)], 0)
    send_in = lat_pad[token_of].reshape(owners, local * cap, width)
    send_grad = (gate_pad[source][:, None] * grad_pad[token_of].astype(jnp.float32)).astype(
        jnp.bfloat16
    )
    send_grad = send_grad.reshape(owners, local * cap, width)
    got_in, got_grad = (
        lax.all_to_all(send_in, "expert", split_axis=0, concat_axis=0, tiled=True),
        lax.all_to_all(send_grad, "expert", split_axis=0, concat_axis=0, tiled=True),
    )
    rows_in = jnp.transpose(got_in.reshape(owners, local, cap, width), (1, 0, 2, 3)).reshape(
        local, owners * cap, width
    )
    rows_grad = jnp.transpose(got_grad.reshape(owners, local, cap, width), (1, 0, 2, 3)).reshape(
        local, owners * cap, width
    )
    w_up = expert_weights[0]
    w_down = expert_weights[1]
    pre = jnp.einsum("jrl,jlf->jrf", rows_in, w_up, preferred_element_type=jnp.float32)
    active = jnp.maximum(pre, 0.0)
    hidden = (active * active).astype(jnp.bfloat16)
    out_part = jnp.einsum("jrf,jlf->jrl", hidden, w_down, preferred_element_type=jnp.float32)
    hid_grad = jnp.einsum("jrl,jlf->jrf", rows_grad, w_down, preferred_element_type=jnp.float32)
    pre_grad = (hid_grad * 2.0 * active).astype(jnp.bfloat16)
    in_part = jnp.einsum("jrf,jlf->jrl", pre_grad, w_up, preferred_element_type=jnp.float32)
    out_sum, in_sum = (
        lax.psum_scatter(
            out_part.astype(jnp.bfloat16), "tensor", scatter_dimension=2, tiled=True
        ).astype(jnp.float32),
        lax.psum_scatter(
            in_part.astype(jnp.bfloat16), "tensor", scatter_dimension=2, tiled=True
        ).astype(jnp.float32),
    )
    out_send = jnp.transpose(
        out_sum.astype(jnp.bfloat16).reshape(local, owners, cap, quarter), (1, 0, 2, 3)
    )
    in_send = jnp.transpose(
        in_sum.astype(jnp.bfloat16).reshape(local, owners, cap, quarter), (1, 0, 2, 3)
    )
    back_out, back_in = (
        lax.all_to_all(out_send, "expert", split_axis=0, concat_axis=0, tiled=True),
        lax.all_to_all(in_send, "expert", split_axis=0, concat_axis=0, tiled=True),
    )
    short_zero = jnp.zeros((1, quarter), jnp.bfloat16)
    out_pad = jnp.concatenate([back_out.reshape(dump, quarter), short_zero], 0)
    in_pad = jnp.concatenate([back_in.reshape(dump, quarter), short_zero], 0)
    weight = jnp.where(kept > 0, gate_weights, 0.0)[..., None]
    keepf = jnp.where(kept > 0, 1.0, 0.0).astype(jnp.float32)[..., None]
    mixed = jnp.sum(weight * out_pad[target].astype(jnp.float32), axis=1).astype(jnp.bfloat16)
    latent_grad = jnp.sum(keepf * in_pad[target].astype(jnp.float32), axis=1).astype(jnp.bfloat16)
    up_term = jnp.einsum("jrl,jrf->jlf", rows_in, pre_grad, preferred_element_type=jnp.float32)
    down_term = jnp.einsum("jrl,jrf->jlf", rows_grad, hidden, preferred_element_type=jnp.float32)
    both_terms = jnp.stack([up_term, down_term], axis=0)
    weight_grads = lax.psum_scatter(
        both_terms.astype(jnp.bfloat16), "dp", scatter_dimension=2, tiled=True
    ).astype(jnp.float32)
    return (mixed, latent_grad, weight_grads)


def solution(mesh):
    in_specs = (
        P(("dp", "expert"), None),
        P(("dp", "expert"), None),
        P(None, "expert", None, "tensor"),
        P(("dp", "expert"), None),
        P(("dp", "expert"), None),
        P(("dp", "expert"), None),
        P(("dp", "expert"), None),
    )
    out_specs = (
        P(("dp", "expert"), "tensor"),
        P(("dp", "expert"), "tensor"),
        P(None, "expert", "dp", "tensor"),
    )
    return jax.shard_map(shards, mesh=mesh, in_specs=in_specs, out_specs=out_specs, check_vma=False)
```

profile of v0, /device:TPU:2, one launch (start us, length us, event | category | flops | bytes accessed | tf_op | source)
XLA Modules:
  0.0 258.8 jit_solution(7820639158043630904)
XLA Ops:
  7.2 0.7 broadcast_select_fusion
  7.9 0.7 compare_select_fusion.1
  8.6 0.1 copy.28
  8.7 0.1 reshape.79
  8.8 4.3 %scatter_custom_fusion = s32[1025]{0:T(1024)S(1)} fusion(s32[1024]{0:T(1024)S(1)} %bitcast.100, s32[1024]{0:T(1024)S(1)} %iota.3, s32[]{:T(128)} %constant.17.clone.1), kind=kCustom, calls=%fused_computation.60 | custom fusion | bytes 4104 | tf_op jit(solution)/shard_map/scatter | solution.py:18
  13.1 1.0 concatenate.15
  14.1 5.3 %gather_fusion = bf16[1024,1024]{1,0:T(8,128)(2,1)} fusion(bf16[129,1024]{1,0:T(8,128)(2,1)S(1)} %concatenate.15, s32[1024]{0:T(1024)S(1)} %get-tuple-element.8), kind=kCustom, calls=%fused_computation | custom fusion | bytes 4198400 | tf_op jit(solution)/shard_map/gather | solution.py:24
  19.5 18.2 %all-to-all-start = ((bf16[64,16,1024]{2,1,0:T(8,128)(2,1)}), bf16[64,16,1024]{2,1,0:T(8,128)(2,1)}, u32[]{:S(2)}, u32[]{:S(2)}) async-start(bf16[64,16,1024]{2,1,0:T(8,128)(2,1)} %bitcast.1), calls=%async_computation | async-start | bytes 4194304 | tf_op jit(solution)/shard_map/all_to_all | solution.py:30
  37.7 0.0 copy-done.6
  37.7 0.1 copy.33
  37.8 0.1 reshape.85
  37.9 0.0 copy-start.5
  37.9 6.2 %gather_fusion.2 = f32[1024]{0:T(1024)S(1)} fusion(f32[1025]{0:T(1024)S(1)} %pad_maximum_fusion.1, s32[1024]{0:T(1024)S(1)} %get-tuple-element.7), kind=kCustom, calls=%fused_computation.2 | custom fusion | bytes 12288 | tf_op jit(solution)/shard_map/gather | solution.py:25
  44.1 0.1 mul.51
  44.2 0.0 copy-done.5
  44.2 4.1 %gather_fusion.3 = bf16[1024,1024]{1,0:T(8,128)(2,1)S(1)} fusion(bf16[129,1024]{1,0:T(8,128)(2,1)S(1)} %concatenate.18, s32[1024]{0:T(1024)S(1)} %get-tuple-element.8), kind=kCustom, calls=%fused_computation.3 | custom fusion | bytes 4198400 | tf_op jit(solution)/shard_map/gather | solution.py:25
  48.3 1.8 fusion
  50.0 35.3 %all-to-all-done = bf16[64,16,1024]{2,1,0:T(8,128)(2,1)} async-done(((bf16[64,16,1024]{2,1,0:T(8,128)(2,1)}), bf16[64,16,1024]{2,1,0:T(8,128)(2,1)}, u32[]{:S(2)}, u32[]{:S(2)}) %all-to-all-start) | async-done | bytes 2097184 | tf_op jit(solution)/shard_map/all_to_all | solution.py:30
  85.3 9.0 %all-to-all-start.2 = ((bf16[64,16,1024]{2,1,0:T(8,128)(2,1)}), bf16[64,16,1024]{2,1,0:T(8,128)(2,1)}, u32[]{:S(2)}, u32[]{:S(2)}) async-start(bf16[64,16,1024]{2,1,0:T(8,128)(2,1)} %fusion), calls=%async_computation.2 | async-start | bytes 4194304 | tf_op jit(solution)/shard_map/all_to_all | solution.py:31
  94.3 0.0 reduce-scatter.10.cloned.1.call-start
  94.3 0.0 copy-done
  94.3 2.3 fusion.25
  96.6 2.1 convolution_convert_fusion.1
  98.7 4.8 %copy.40 = bf16[2,512,1024]{1,0,2:T(2,128)(2,1)S(1)} copy(bf16[2,512,1024]{2,1,0:T(8,128)(2,1)} %convolution_convert_fusion.1) | data formatting | bytes 4194304
  103.5 1.9 copy.44
  105.4 0.0 reduce-scatter.10.cloned.1.call-update
  105.5 0.0 reduce-scatter.12.cloned.1.call-start
  105.5 39.4 %all-to-all-done.2 = bf16[64,16,1024]{2,1,0:T(8,128)(2,1)} async-done(((bf16[64,16,1024]{2,1,0:T(8,128)(2,1)}), bf16[64,16,1024]{2,1,0:T(8,128)(2,1)}, u32[]{:S(2)}, u32[]{:S(2)}) %all-to-all-start.2) | async-done | bytes 2097184 | tf_op jit(solution)/shard_map/all_to_all | solution.py:31
  144.9 0.0 copy-done.1
  144.9 2.5 fusion.34
  147.4 0.0 copy-start.3
  147.4 0.8 copy-done.3
  148.2 0.0 copy-done.2
  148.2 0.7 convolution_convert_fusion
  149.0 4.0 %copy.42 = bf16[2,512,1024]{1,0,2:T(2,128)(2,1)} copy(bf16[2,512,1024]{2,1,0:T(8,128)(2,1)S(1)} %convolution_convert_fusion) | data formatting | bytes 4194304
  153.0 3.5 %copy.45 = bf16[128,8,2,512]{3,1,2,0:T(8,128)(2,1)} copy(bf16[128,8,2,512]{3,2,1,0:T(2,128)(2,1)} %bitcast.95) | data formatting | bytes 4194304
  156.5 0.0 reduce-scatter.12.cloned.1.call-update
  156.6 0.0 reduce-scatter.8.cloned.1.call-start
  156.6 1.0 copy-done.4
  157.6 2.5 fusion.22
  160.1 2.5 fusion.19
  162.7 1.5 pad_maximum_fusion
  164.2 0.0 reduce-scatter.8.cloned.1.call-update
  164.2 1.8 reduce-scatter.10.cloned.1.call-done
  166.0 1.1 reshape.149
  167.1 0.2 copy.41
  167.4 0.8 copy_bitcast_fusion.1
  168.2 13.4 %all-to-all-start.1 = ((bf16[64,2,8,128]{3,2,1,0:T(8,128)(2,1)}), bf16[64,2,8,128]{3,2,1,0:T(8,128)(2,1)S(1)}, u32[]{:S(2)}, u32[]{:S(2)}) async-start(bf16[64,2,8,128]{3,2,1,0:T(8,128)(2,1)} %copy_bitcast_fusion.1), calls=%async_computation.1 | async-start | bytes 524288 | tf_op jit(solution)/shard_map/all_to_all | solution.py:63
  181.5 35.0 %reduce-scatter.12.cloned.1.call-done = bf16[128,1024]{1,0:T(8,128)(2,1)} async-done(((bf16[1024,1024]{1,0:T(8,128)(2,1)}), bf16[128,1024]{1,0:T(8,128)(2,1)}) %reduce-scatter.12.cloned.1.call-update) | async-done | bytes 262160
  216.5 1.1 reshape.151
  217.7 0.2 copy.43
  217.9 0.8 copy_bitcast_fusion
  218.7 0.0 all-to-all-done.1
  218.7 13.1 %all-to-all-start.3 = ((bf16[64,2,8,128]{3,2,1,0:T(8,128)(2,1)}), bf16[64,2,8,128]{3,2,1,0:T(8,128)(2,1)S(1)}, u32[]{:S(2)}, u32[]{:S(2)}) async-start(bf16[64,2,8,128]{3,2,1,0:T(8,128)(2,1)} %copy_bitcast_fusion), calls=%async_computation.3 | async-start | bytes 524288 | tf_op jit(solution)/shard_map/all_to_all | solution.py:64
  231.7 0.1 copy.31
  231.8 0.1 reshape.101
  232.0 0.1 copy.27
  232.1 0.1 copy.32
  232.2 6.2 %reduce-scatter.8.cloned.1.call-done = bf16[2,2,512,256]{3,2,1,0:T(8,128)(2,1)} async-done(((bf16[2,2,1024,256]{3,2,1,0:T(8,128)(2,1)}), bf16[2,2,512,256]{3,2,1,0:T(8,128)(2,1)}) %reduce-scatter.8.cloned.1.call-update) | async-done | bytes 1048592 | tf_op jit(solution)/shard_map/reduce_scatter | solution.py:76
  238.4 2.7 %convert_element_type.54 = f32[2,2,512,256]{3,2,1,0:T(8,128)} convert(bf16[2,2,512,256]{3,2,1,0:T(8,128)(2,1)} %reduce-scatter.8.cloned.1.call-done) | non-fusion elementwise | flops 524288 | bytes 3145728 | tf_op jit(solution)/shard_map/convert_element_type | solution.py:78
  241.1 3.7 %all-to-all-done.3 = bf16[64,2,8,128]{3,2,1,0:T(8,128)(2,1)S(1)} async-done(((bf16[64,2,8,128]{3,2,1,0:T(8,128)(2,1)}), bf16[64,2,8,128]{3,2,1,0:T(8,128)(2,1)S(1)}, u32[]{:S(2)}, u32[]{:S(2)}) %all-to-all-start.3) | async-done | bytes 262176 | tf_op jit(solution)/shard_map/all_to_all | solution.py:64
  244.8 3.2 %gather_fusion.1 = bf16[1024,128]{1,0:T(8,128)(2,1)S(1)} fusion(bf16[1025,128]{1,0:T(8,128)(2,1)S(1)} %concatenate.16, s32[1024]{0:T(1024)S(1)} %broadcast_clamp_fusion), kind=kCustom, calls=%fused_computation.1 | custom fusion | bytes 528384 | tf_op jit(solution)/shard_map/gather | solution.py:71
  248.0 3.2 %gather_fusion.4 = bf16[1024,128]{1,0:T(8,128)(2,1)S(1)} fusion(bf16[1025,128]{1,0:T(8,128)(2,1)S(1)} %concatenate.19, s32[1024]{0:T(1024)S(1)} %broadcast_clamp_fusion), kind=kCustom, calls=%fused_computation.4 | custom fusion | bytes 528384 | tf_op jit(solution)/shard_map/gather | solution.py:72
  251.3 1.0 fusion.45
  (14 shorter events, 0.1 us)
Async XLA Ops:
  19.5 18.2 %copy-start.6 = (f32[128,8]{0,1:T(8,128)S(1)}, f32[128,8]{0,1:T(8,128)}, u32[]{:S(2)}) copy-start(f32[128,8]{0,1:T(8,128)} %param.13) | copy-start | bytes 12292
  19.5 65.8 %all-to-all-start = ((bf16[64,16,1024]{2,1,0:T(8,128)(2,1)}), bf16[64,16,1024]{2,1,0:T(8,128)(2,1)}, u32[]{:S(2)}, u32[]{:S(2)}) async-start(bf16[64,16,1024]{2,1,0:T(8,128)(2,1)} %bitcast.1), calls=%async_computation | async-start | bytes 4194304 | tf_op jit(solution)/shard_map/all_to_all | solution.py:30
  37.9 6.2 %copy-start.5 = (bf16[128,1024]{1,0:T(8,128)(2,1)S(1)}, bf16[128,1024]{1,0:T(8,128)(2,1)}, u32[]{:S(2)}) copy-start(bf16[128,1024]{1,0:T(8,128)(2,1)} %param.8) | copy-start | bytes 786436
  50.0 44.3 %copy-start = (bf16[2,2,1024,256]{3,2,1,0:T(8,128)(2,1)S(1)}, bf16[2,2,1024,256]{3,2,1,0:T(8,128)(2,1)}, u32[]{:S(2)}) copy-start(bf16[2,2,1024,256]{3,2,1,0:T(8,128)(2,1)} %param.9) | copy-start | bytes 6291460
  85.3 59.6 %all-to-all-start.2 = ((bf16[64,16,1024]{2,1,0:T(8,128)(2,1)}), bf16[64,16,1024]{2,1,0:T(8,128)(2,1)}, u32[]{:S(2)}, u32[]{:S(2)}) async-start(bf16[64,16,1024]{2,1,0:T(8,128)(2,1)} %fusion), calls=%async_computation.2 | async-start | bytes 4194304 | tf_op jit(solution)/shard_map/all_to_all | solution.py:31
  94.3 71.7 %reduce-scatter.10.cloned.1.call-start = ((), (), s32[]{:S(2)}) async-start(), calls=%async_computation.8 | async-start | bytes 2359296
  105.4 39.5 %copy-start.1 = (bf16[2,2,1024,256]{3,2,1,0:T(8,128)(2,1)S(1)}, bf16[2,2,1024,256]{3,2,1,0:T(8,128)(2,1)}, u32[]{:S(2)}) copy-start(bf16[2,2,1024,256]{3,2,1,0:T(8,128)(2,1)} %param.9) | copy-start | bytes 6291460
  105.5 111.1 %reduce-scatter.12.cloned.1.call-start = ((), (), s32[]{:S(2)}) async-start(), calls=%async_computation.9 | async-start | bytes 2359296
  144.9 3.3 %copy-start.2 = (bf16[2,2,1024,256]{3,2,1,0:T(8,128)(2,1)S(1)}, bf16[2,2,1024,256]{3,2,1,0:T(8,128)(2,1)}, u32[]{:S(2)}) copy-start(bf16[2,2,1024,256]{3,2,1,0:T(8,128)(2,1)} %param.9) | copy-start | bytes 6291460
  147.4 0.8 copy-start.3
  156.5 1.0 copy-start.4
  156.6 81.8 %reduce-scatter.8.cloned.1.call-start = ((), (), s32[]{:S(2)}) async-start(), calls=%async_computation.7 | async-start | bytes 3145728 | tf_op jit(solution)/shard_map/reduce_scatter | solution.py:76
  168.2 50.5 %all-to-all-start.1 = ((bf16[64,2,8,128]{3,2,1,0:T(8,128)(2,1)}), bf16[64,2,8,128]{3,2,1,0:T(8,128)(2,1)S(1)}, u32[]{:S(2)}, u32[]{:S(2)}) async-start(bf16[64,2,8,128]{3,2,1,0:T(8,128)(2,1)} %copy_bitcast_fusion.1), calls=%async_computation.1 | async-start | bytes 524288 | tf_op jit(solution)/shard_map/all_to_all | solution.py:63
  218.7 26.1 %all-to-all-start.3 = ((bf16[64,2,8,128]{3,2,1,0:T(8,128)(2,1)}), bf16[64,2,8,128]{3,2,1,0:T(8,128)(2,1)S(1)}, u32[]{:S(2)}, u32[]{:S(2)}) async-start(bf16[64,2,8,128]{3,2,1,0:T(8,128)(2,1)} %copy_bitcast_fusion), calls=%async_computation.3 | async-start | bytes 524288 | tf_op jit(solution)/shard_map/all_to_all | solution.py:64
Sparse Core Ops, SparseCore 0:
  105.6 60.3 reduce-scatter.9
  169.4 47.0 reduce-scatter.11
  220.5 17.8 reduce-scatter.7
where the time goes:
time: 260 us; the launch traced here: 259 us
  waiting for transfers between devices  121 us (47%)
  starting transfers between devices  53.7 us (21%)
  local copies, waits for them, and re-layouts  48.6 us (19%)
  between operations  14 us (5%)
  matrix products  12.7 us (5%)
  other arithmetic  8.44 us (3%)
    all_to_all x1, waiting for transfers between devices, shards(): lax.all_to_all(send_grad, 'expert', split_axis=0, concat_axis=0, tiled=True)  39.4 us
    unnamed x5, waiting for transfers between devices  36.9 us
    all_to_all x1, waiting for transfers between devices, shards(): lax.all_to_all(send_in, 'expert', split_axis=0, concat_axis=0, tiled=True)  35.3 us
    unnamed x23, local copies, waits for them, and re-layouts  18.9 us
    all_to_all x1, starting transfers between devices, shards(): lax.all_to_all(send_in, 'expert', split_axis=0, concat_axis=0, tiled=True)  18.2 us
    all_to_all x1, starting transfers between devices, shards(): lax.all_to_all(out_send, 'expert', split_axis=0, concat_axis=0, tiled=True)  13.4 us
    all_to_all x1, starting transfers between devices, shards(): lax.all_to_all(in_send, 'expert', split_axis=0, concat_axis=0, tiled=True)  13.1 us
    all_to_all x1, starting transfers between devices, shards(): lax.all_to_all(send_grad, 'expert', split_axis=0, concat_axis=0, tiled=True)  8.97 us
  transfers between devices with their start and end apart: 7, of which 6 were waited for; matrix products, arithmetic and copies ran while one was open for 19% of the time, Pallas kernels for 0%

commit v1 on v0

v1 whole, which is shorter than its diff:
```python
import jax
import jax.numpy as jnp
from jax import lax
from jax.experimental import pallas as pl
from jax.experimental.pallas import tpu as pltpu
from jax.sharding import PartitionSpec as P

SIDE = 8
RING = 8
PARTS = 4
CAP = 8
LOCAL = 2
SLICE = 128
ROWS = 128
STEPS_Y = (0, 4, 1, 7, 2, 6, 3, 5)
MESH = pl.DeviceIdType.MESH
BF16 = jnp.bfloat16
F32 = jnp.float32


def contract(left, right, dim_left, dim_right):
    return lax.dot_general(
        left, right, (((dim_left,), (dim_right,)), ((), ())), preferred_element_type=F32
    )


def block_kernel(
    ids, slot, kept, gate, lat_hbm, grad_hbm, w_hbm,
    mixed, lat_grad, own_terms, got_terms,
    lat, grad, w, mask, gate_hi, gate_lo,
    outgoing, incoming, rows, partial, sums, back, returned, hidden, pre_grad, keep_half, send_half,
    load_sem, out_send, out_recv, gather_send, gather_recv, sum_send, sum_recv,
    back_send, back_recv, term_send, term_recv, keep_sem,
):
    dp = lax.axis_index("dp")
    chip = lax.axis_index("expert")
    z = lax.axis_index("tensor")
    y, x = lax.div(chip, SIDE), lax.rem(chip, SIDE)
    peers = SIDE * SIDE
    slots = peers * LOCAL * CAP
    above, below = lax.rem(z + 1, RING), lax.rem(z + RING - 1, RING)

    barrier = pltpu.get_barrier_semaphore()

    def greet(step, carry):
        pl.semaphore_signal(
            barrier, inc=1, device_id={"expert": lax.rem(chip + step, peers)}, device_id_type=MESH
        )
        return carry

    loads = [
        pltpu.make_async_copy(lat_hbm.at[:, pl.ds(pl.multiple_of(z * SLICE, SLICE), SLICE)], lat, load_sem.at[0]),
        pltpu.make_async_copy(grad_hbm.at[:, pl.ds(pl.multiple_of(z * SLICE, SLICE), SLICE)], grad, load_sem.at[1]),
        pltpu.make_async_copy(w_hbm, w, load_sem.at[2]),
    ]
    for load in loads:
        load.start()
    lax.fori_loop(1, peers, greet, 0)
    pl.semaphore_signal(barrier, inc=1, device_id={"tensor": above}, device_id_type=MESH)
    pl.semaphore_signal(barrier, inc=1, device_id={"tensor": below}, device_id_type=MESH)
    pl.semaphore_signal(barrier, inc=1, device_id={"dp": 1 - dp}, device_id_type=MESH)

    target = jnp.where(kept[...] > 0, ids[...] * CAP + slot[...], slots)
    gates = gate[...]
    loads[0].wait()
    loads[1].wait()

    def build(step, carry):
        first = pl.multiple_of(step * 128, 128)
        slot_of = first + lax.broadcasted_iota(jnp.int32, (128, 128), 0)
        placed = jnp.zeros((128, 128), F32)
        weight = jnp.zeros((128, 128), F32)
        for k in range(ids.shape[0]):
            same = target[k : k + 1, :] == slot_of
            placed = jnp.where(same, 1.0, placed)
            weight = jnp.where(same, gates[k : k + 1, :], weight)
        hi = weight.astype(BF16)
        here = pl.ds(first, 128)
        mask[here, :] = placed.astype(BF16)
        gate_hi[here, :] = hi
        gate_lo[here, :] = (weight - hi.astype(F32)).astype(BF16)
        onehot = placed.astype(BF16)
        scale = jnp.sum(weight, axis=1, keepdims=True)
        lat_rows = contract(onehot, lat[...], 1, 0).astype(BF16)
        grad_rows = (scale * contract(onehot, grad[...], 1, 0)).astype(BF16)
        dests = pl.ds(pl.multiple_of(step * 8, 8), 8)
        outgoing[dests, 0:16, :] = lat_rows.reshape(8, 16, SLICE)
        outgoing[dests, 16:32, :] = grad_rows.reshape(8, 16, SLICE)
        return carry

    lax.fori_loop(0, slots // 128, build, 0)
    pl.semaphore_wait(barrier, peers - 1 + 3)

    def dispatch(part):
        for half in range(2):
            index = 2 * part + half
            row = lax.rem(y + STEPS_Y[index], SIDE) * SIDE

            def send(step, carry):
                dest = row + lax.rem(x + step, SIDE)
                pltpu.make_async_remote_copy(
                    src_ref=outgoing.at[dest], dst_ref=incoming.at[index * SIDE + step],
                    send_sem=out_send, recv_sem=out_recv.at[part],
                    device_id={"expert": dest}, device_id_type=MESH,
                ).start()
                return carry

            lax.fori_loop(1 if index == 0 else 0, SIDE, send, 0)

    def wait_bytes(ref, sem):
        pltpu.make_async_copy(ref, ref, sem).wait()

    def hop(part, way, step, start):
        if way == 0:
            owner, to = lax.rem(z + RING - (step - 1), RING), above
            landed = lax.rem(z + RING - step, RING)
        else:
            owner, to = lax.rem(z + step - 1, RING), below
            landed = lax.rem(z + step, RING)
        source, dest = rows.at[part, owner], rows.at[part, landed]
        if step == RING // 2:
            source, dest = rows.at[part, owner, way], rows.at[part, landed, way]
        copy = pltpu.make_async_remote_copy(
            src_ref=source, dst_ref=source if start else dest,
            send_sem=gather_send.at[part, way, step - 1],
            recv_sem=gather_recv.at[part, way, step - 1],
            device_id={"tensor": to}, device_id_type=MESH,
        )
        return copy

    def enter(part):
        first = part * 2 * SIDE
        if part == 0:
            incoming[0] = outgoing[chip]
            wait_bytes(incoming.at[pl.ds(1, 2 * SIDE - 1)], out_recv.at[part])
        else:
            wait_bytes(incoming.at[pl.ds(first, 2 * SIDE)], out_recv.at[part])
        got = incoming[pl.ds(first, 2 * SIDE)].astype(F32).reshape(2 * SIDE, 4, CAP, SLICE)
        for kind in range(2):
            for local in range(LOCAL):
                rows[part, z, kind, local] = (
                    got[:, 2 * kind + local].reshape(ROWS, SLICE).astype(BF16)
                )
        for way in range(2):
            hop(part, way, 1, True).start()

    def forward(part, step):
        for way in range(2):
            hop(part, way, step - 1, False).wait_recv()
            hop(part, way, step, True).start()

    def experts(part):
        for way in range(2):
            hop(part, way, RING // 2, False).wait_recv()

        def one(local, carry):
            got_in = jnp.concatenate([rows[part, q, 0, local] for q in range(RING)], axis=1)
            got_grad = jnp.concatenate([rows[part, q, 1, local] for q in range(RING)], axis=1)
            active = jnp.maximum(contract(got_in, w[0, local], 1, 0), 0.0)
            unit = (active * active).astype(BF16)
            unit_grad = (contract(got_grad, w[1, local], 1, 0) * 2.0 * active).astype(BF16)
            here = pl.ds(part * ROWS, ROWS)
            hidden[local, here, :] = unit
            pre_grad[local, here, :] = unit_grad
            for q in range(0, RING, 2):
                cols = pl.ds(q * SLICE, 2 * SLICE)
                out_cols = contract(unit, w[1, local, cols, :], 1, 1).astype(BF16)
                in_cols = contract(unit_grad, w[0, local, cols, :], 1, 1).astype(BF16)
                for side in range(2):
                    span = slice(side * SLICE, (side + 1) * SLICE)
                    partial[part, q + side, 0, local] = out_cols[:, span]
                    partial[part, q + side, 1, local] = in_cols[:, span]
            return carry

        lax.fori_loop(0, LOCAL, one, 0)

    def sum_hop(part, way, step):
        ahead = RING // 2 + 1 - step
        owner = lax.rem(z + ahead, RING) if way == 0 else lax.rem(z + RING - ahead, RING)
        source, dest = partial.at[part, owner], sums.at[part, way, step - 1]
        if step == 1:
            source, dest = partial.at[part, owner, way], sums.at[part, way, 0, way]
        copy = pltpu.make_async_remote_copy(
            src_ref=source, dst_ref=dest,
            send_sem=sum_send.at[part, way, step - 1],
            recv_sem=sum_recv.at[part, way, step - 1],
            device_id={"tensor": above if way == 0 else below}, device_id_type=MESH,
        )
        return owner, copy

    def add(part, step):
        for way in range(2):
            owner, copy = sum_hop(part, way, step)
            if step > 1:
                sum_hop(part, way, step - 1)[1].wait_recv()
                for kind in (range(2) if step > 2 else (way,)):
                    for local in range(LOCAL):
                        partial[part, owner, kind, local] = (
                            partial[part, owner, kind, local].astype(F32)
                            + sums[part, way, step - 2, kind, local].astype(F32)
                        ).astype(BF16)
            copy.start()

    def give_back(part):
        for way in range(2):
            sum_hop(part, way, RING // 2)[1].wait_recv()
        pieces = []
        for kind in range(2):
            for local in range(LOCAL):
                total = (
                    partial[part, z, kind, local].astype(F32)
                    + sums[part, 0, RING // 2 - 1, kind, local].astype(F32)
                    + sums[part, 1, RING // 2 - 1, kind, local].astype(F32)
                )
                pieces.append(total.reshape(2 * SIDE, CAP, SLICE))
        back[pl.ds(part * 2 * SIDE, 2 * SIDE)] = jnp.concatenate(pieces, axis=1).astype(BF16)
        for half in range(2):
            index = 2 * part + half
            row = lax.rem(y + SIDE - STEPS_Y[index], SIDE) * SIDE

            def send(step, carry):
                dest = row + lax.rem(x + SIDE - step, SIDE)
                pltpu.make_async_remote_copy(
                    src_ref=back.at[index * SIDE + step], dst_ref=returned.at[chip],
                    send_sem=back_send, recv_sem=back_recv,
                    device_id={"expert": dest}, device_id_type=MESH,
                ).start()
                return carry

            lax.fori_loop(1 if index == 0 else 0, SIDE, send, 0)

    def terms(kind, mine):
        half = dp if mine else 1 - dp
        store = keep_half if mine else send_half
        other = pre_grad if kind == 0 else hidden

        def one(step, carry):
            local, q = lax.div(step, RING // 2), lax.rem(step, RING // 2)
            left = jnp.concatenate(
                [rows[part, half * (RING // 2) + q, kind, local] for part in range(PARTS)], axis=0
            )
            span = pl.ds(pl.multiple_of(q * SLICE, SLICE), SLICE)
            store[kind, local, span, :] = contract(left, other[local], 0, 0).astype(BF16)
            return carry

        lax.fori_loop(0, LOCAL * (RING // 2), one, 0)

    term_copy = pltpu.make_async_remote_copy(
        src_ref=send_half, dst_ref=got_terms, send_sem=term_send, recv_sem=term_recv,
        device_id={"dp": 1 - dp}, device_id_type=MESH,
    )
    keep_copy = pltpu.make_async_copy(keep_half, own_terms, keep_sem)

    for part in range(PARTS):
        dispatch(part)
    enter(0)
    enter(1)
    for step in (2, 3, 4):
        forward(0, step)
        forward(1, step)
    enter(2)
    enter(3)
    loads[2].wait()
    experts(0)
    forward(2, 2)
    experts(1)
    forward(3, 2)
    forward(2, 3)
    forward(3, 3)
    forward(2, 4)
    forward(3, 4)
    add(0, 1)
    add(1, 1)
    add(0, 2)
    add(1, 2)
    experts(2)
    add(0, 3)
    experts(3)
    add(1, 3)
    add(0, 4)
    add(1, 4)
    add(2, 1)
    add(3, 1)
    terms(0, False)
    add(2, 2)
    give_back(0)
    add(3, 2)
    terms(1, False)
    term_copy.start()
    give_back(1)
    add(2, 3)
    terms(0, True)
    add(3, 3)
    terms(1, True)
    keep_copy.start()
    add(2, 4)
    add(3, 4)
    give_back(2)
    give_back(3)

    returned[chip] = back[0]
    wait_bytes(returned.at[pl.ds(0, peers - 1)], back_recv)
    out_rows = returned[:, 0:16, :].reshape(slots, SLICE)
    in_rows = returned[:, 16:32, :].reshape(slots, SLICE)
    mixed[...] = (contract(gate_hi[...], out_rows, 0, 0) + contract(gate_lo[...], out_rows, 0, 0)).astype(BF16)
    lat_grad[...] = contract(mask[...], in_rows, 0, 0).astype(BF16)

    term_copy.wait()
    keep_copy.wait()
    wait_bytes(outgoing.at[pl.ds(0, peers - 1)], out_send)
    wait_bytes(back.at[pl.ds(0, peers - 1)], back_send)
    for part in range(PARTS):
        for way in range(2):
            for step in range(1, RING // 2 + 1):
                hop(part, way, step, True).wait_send()
                sum_hop(part, way, step)[1].wait_send()


def shards(latent, grad_out, expert_weights, expert_ids, slot_index, kept, gate_weights):
    tokens, width = latent.shape
    units = expert_weights.shape[3]
    peers = lax.axis_size("expert")
    slots = peers * LOCAL * CAP
    half = width // 2
    vmem = pl.BlockSpec(memory_space=pltpu.VMEM)
    anywhere = pl.BlockSpec(memory_space=pl.ANY)
    dma = pltpu.SemaphoreType.DMA
    ring = (PARTS, 2, RING // 2)
    mixed, lat_grad, own, got = pl.pallas_call(
        block_kernel,
        out_shape=(
            jax.ShapeDtypeStruct((tokens, SLICE), BF16),
            jax.ShapeDtypeStruct((tokens, SLICE), BF16),
            jax.ShapeDtypeStruct((2, LOCAL, half, units), BF16),
            jax.ShapeDtypeStruct((2, LOCAL, half, units), BF16),
        ),
        in_specs=[vmem] * 4 + [anywhere] * 3,
        out_specs=(vmem, vmem, anywhere, anywhere),
        scratch_shapes=[
            pltpu.VMEM((tokens, SLICE), BF16),
            pltpu.VMEM((tokens, SLICE), BF16),
            pltpu.VMEM((2, LOCAL, width, units), BF16),
            pltpu.VMEM((slots, tokens), BF16),
            pltpu.VMEM((slots, tokens), BF16),
            pltpu.VMEM((slots, tokens), BF16),
            pltpu.VMEM((peers, 32, SLICE), BF16),
            pltpu.VMEM((peers, 32, SLICE), BF16),
            pltpu.VMEM((PARTS, RING, 2, LOCAL, ROWS, SLICE), BF16),
            pltpu.VMEM((PARTS, RING, 2, LOCAL, ROWS, SLICE), BF16),
            pltpu.VMEM(ring + (2, LOCAL, ROWS, SLICE), BF16),
            pltpu.VMEM((peers, 32, SLICE), BF16),
            pltpu.VMEM((peers, 32, SLICE), BF16),
            pltpu.VMEM((LOCAL, PARTS * ROWS, units), BF16),
            pltpu.VMEM((LOCAL, PARTS * ROWS, units), BF16),
            pltpu.VMEM((2, LOCAL, half, units), BF16),
            pltpu.VMEM((2, LOCAL, half, units), BF16),
            dma((3,)),
            dma,
            dma((PARTS,)),
            dma(ring),
            dma(ring),
            dma(ring),
            dma(ring),
            dma,
            dma,
            dma,
            dma,
            dma,
        ],
        compiler_params=pltpu.CompilerParams(
            collective_id=0, has_side_effects=True, vmem_limit_bytes=40 * 2**20
        ),
    )(expert_ids.T, slot_index.T, kept.T, gate_weights.T, latent, grad_out, expert_weights)
    return (mixed, lat_grad, own.astype(F32) + got.astype(F32))


def solution(mesh):
    in_specs = (
        P(("dp", "expert"), None),
        P(("dp", "expert"), None),
        P(None, "expert", None, "tensor"),
        P(("dp", "expert"), None),
        P(("dp", "expert"), None),
        P(("dp", "expert"), None),
        P(("dp", "expert"), None),
    )
    out_specs = (
        P(("dp", "expert"), "tensor"),
        P(("dp", "expert"), "tensor"),
        P(None, "expert", "dp", "tensor"),
    )
    return jax.shard_map(shards, mesh=mesh, in_specs=in_specs, out_specs=out_specs, check_vma=False)
```

time: 260 us -> 137 us (0.53)
  Pallas kernels: 0 us -> 127 us
  waiting for transfers between devices: 121 us -> 0 us
  starting transfers between devices: 53.7 us -> 0 us
  local copies, waits for them, and re-layouts: 48.6 us -> 7.46 us
  between operations: 14 us -> 0.66 us
  matrix products: 12.7 us -> 0 us
  other arithmetic: 8.44 us -> 1.56 us
    pallas_call x0 -> x1, Pallas kernels: none -> 127 us  [shards(): pl.pallas_call(block_kernel, out_shape=(jax.ShapeDtypeStruct((tokens, SLI...]
    all_to_all x4 -> x0, waiting for transfers between devices: 78.4 us -> none  [the longest x1 39.4 us: shards(): lax.all_to_all(send_grad, 'expert', split_axis=0, concat_axis=0, tiled=True)]
    all_to_all x4 -> x0, starting transfers between devices: 53.6 us -> none  [the longest x1 18.2 us: shards(): lax.all_to_all(send_in, 'expert', split_axis=0, concat_axis=0, tiled=True)]
    unnamed x5 -> x0, waiting for transfers between devices: 36.9 us -> none
    gather x5 -> x0, local copies, waits for them, and re-layouts: 22 us -> none  [the longest x1 6.15 us: shards(): gate_pad[source][:, None] * grad_pad[token_of].astype(jnp.float32)]
    dot_general x6 -> x0, matrix products: 12.7 us -> none  [the longest x1 2.55 us: shards(): jnp.einsum('jrl,jrf->jlf', rows_in, pre_grad, preferred_element_type=jnp....]
    unnamed x23 -> x16, local copies, waits for them, and re-layouts: 18.9 us -> 7.46 us
    reduce_scatter x1 -> x0, waiting for transfers between devices: 6.2 us -> none  [shards(): lax.psum_scatter(both_terms.astype(jnp.bfloat16), 'dp', scatter_dimension...]
  transfers between devices with their start and end apart: 7 -> 0, of which waited for: 6 -> 0; matrix products, arithmetic and copies ran while one was open for 19% -> 0% of each run, Pallas kernels for 0% -> 0%
where the time goes in v1:
time: 137 us
  Pallas kernels  127 us (93%)
  local copies, waits for them, and re-layouts  7.46 us (5%)
  other arithmetic  1.56 us (1%)
    pallas_call x1, Pallas kernels, shards(): pl.pallas_call(block_kernel, out_shape=(jax.ShapeDtypeStruct((tokens, SLI...  127 us
    unnamed x16, local copies, waits for them, and re-layouts  7.46 us

profile of v1, /device:TPU:2, one launch (start us, length us, event | category | flops | bytes accessed | tf_op | source)
XLA Modules:
  0.0 136.5 jit_solution(16971075549508621368)
XLA Ops:
  0.6 0.0 copy-start
  0.6 1.6 %copy-done = bf16[2,2,1024,256]{3,2,1,0:T(8,128)(2,1)S(1)} copy-done((bf16[2,2,1024,256]{3,2,1,0:T(8,128)(2,1)S(1)}, bf16[2,2,1024,256]{3,2,1,0:T(8,128)(2,1)}, u32[]{:S(2)}) %copy-start) | copy-done | bytes 2097176
  2.2 0.0 copy-start.1
  2.2 0.9 copy-done.1
  3.2 0.0 copy-start.2
  3.2 0.9 copy-done.2
  4.1 0.0 copy-start.3
  4.1 0.7 copy-done.3
  4.8 0.0 copy-start.4
  4.8 0.7 copy-done.4
  5.5 0.0 copy-start.5
  5.5 0.7 copy-done.5
  6.2 0.0 copy-start.6
  6.2 0.7 copy-done.6
  6.9 126.9 %shard_map.94 = (bf16[128,128]{1,0:T(8,128)(2,1)S(1)}, bf16[128,128]{1,0:T(8,128)(2,1)S(1)}, bf16[2,2,512,256]{3,2,1,0:T(8,128)(2,1)S(1)}, bf16[2,2,512,256]{3,2,1,0:T(8,128)(2,1)S(1)}) custom-call(s32[8,128]{1,0:T(8,128)S(1)} %bitcast.4, s32[8,128]{1,0:T(8,128)S(1)} %bitcast.5, s32[8,128]{1,0:T(8,128)S(1)} %bitcast.6, f32[8,128]{1,0:T(8,128)S(1)} %bitcast.7, ...), custom_call_target="tpu_custom_call" | custom-call | tf_op jit(solution)/shard_map/pallas_call | solution.py:329
  133.7 1.6 %convert_add_fusion = f32[2,2,512,256]{3,2,1,0:T(8,128)} fusion(bf16[2,2,512,256]{3,2,1,0:T(8,128)(2,1)S(1)} %get-tuple-element.10, bf16[2,2,512,256]{3,2,1,0:T(8,128)(2,1)S(1)} %get-tuple-element.9), kind=kLoop, calls=%fused_computation | loop fusion | flops 1572864 | bytes 4194304 | tf_op jit(solution)/shard_map/add | solution.py:374
  135.3 0.6 copy.12
  135.9 0.6 copy.13
Async XLA Ops:
  0.6 1.6 %copy-start = (bf16[2,2,1024,256]{3,2,1,0:T(8,128)(2,1)S(1)}, bf16[2,2,1024,256]{3,2,1,0:T(8,128)(2,1)}, u32[]{:S(2)}) copy-start(bf16[2,2,1024,256]{3,2,1,0:T(8,128)(2,1)} %w_hbm.1) | copy-start | bytes 6291460
  2.2 0.9 copy-start.1
  3.2 0.9 copy-start.2
  4.1 0.7 copy-start.3
  4.8 0.7 copy-start.4
  5.5 0.7 copy-start.5
  6.2 0.7 copy-start.6

commit v2 on v1

v2 whole, which is shorter than its diff:
```python
import jax
import jax.numpy as jnp
from jax import lax
from jax.experimental import pallas as pl
from jax.experimental.pallas import tpu as pltpu
from jax.sharding import PartitionSpec as P

SIDE = 8
RING = 8
STEPS = 3
PARTS = 4
CAP = 8
LOCAL = 2
SLICE = 128
ROWS = 128
STEPS_Y = (0, 4, 1, 7, 2, 6, 3, 5)
MESH = pl.DeviceIdType.MESH
BF16 = jnp.bfloat16
F32 = jnp.float32


def contract(left, right, dim_left, dim_right):
    return lax.dot_general(
        left, right, (((dim_left,), (dim_right,)), ((), ())), preferred_element_type=F32
    )


def block_kernel(
    ids_hbm, slot_hbm, kept_hbm, gate_hbm, lat_hbm, grad_hbm, w_hbm,
    mixed, lat_grad, own_terms, got_terms,
    ids, slot, kept, gate, lat, grad, w, mask, gate_hi, gate_lo,
    outgoing, incoming, rows, partial, sums, back, returned, far_send, far_got, hidden, pre_grad, keep_half, send_half,
    load_sem, out_send, out_recv, gather_send, gather_recv, sum_send, sum_recv,
    back_send, back_recv, far_sems, term_send, term_recv, keep_sem, row_here,
):
    dp = lax.axis_index("dp")
    chip = lax.axis_index("expert")
    z = lax.axis_index("tensor")
    y, x = lax.div(chip, SIDE), lax.rem(chip, SIDE)
    peers = SIDE * SIDE
    slots = peers * LOCAL * CAP
    above, below = lax.rem(z + 1, RING), lax.rem(z + RING - 1, RING)

    across = lax.rem(z + RING // 2, RING)
    span = pl.ds(pl.multiple_of(z * SLICE, SLICE), SLICE)
    far_span = pl.ds(pl.multiple_of(across * SLICE, SLICE), SLICE)
    barrier = pltpu.get_barrier_semaphore()

    def greet(step, carry):
        pl.semaphore_signal(
            barrier, inc=1, device_id={"expert": y * SIDE + lax.rem(x + step, SIDE)}, device_id_type=MESH
        )
        pl.semaphore_signal(
            barrier, inc=1, device_id={"expert": lax.rem(y + step, SIDE) * SIDE + x}, device_id_type=MESH
        )
        return carry

    def vouch(step, carry):
        pl.semaphore_signal(
            row_here, inc=1, device_id={"expert": lax.rem(y + step, SIDE) * SIDE + x}, device_id_type=MESH
        )
        return carry

    lax.fori_loop(1, SIDE, greet, 0)
    for position in (above, below, across):
        pl.semaphore_signal(barrier, inc=1, device_id={"tensor": position}, device_id_type=MESH)
    pl.semaphore_signal(barrier, inc=1, device_id={"dp": 1 - dp}, device_id_type=MESH)

    loads = [
        pltpu.make_async_copy(ids_hbm, ids, load_sem.at[0]),
        pltpu.make_async_copy(slot_hbm, slot, load_sem.at[1]),
        pltpu.make_async_copy(kept_hbm, kept, load_sem.at[2]),
        pltpu.make_async_copy(gate_hbm, gate, load_sem.at[3]),
        pltpu.make_async_copy(lat_hbm.at[:, span], lat.at[0], load_sem.at[4]),
        pltpu.make_async_copy(grad_hbm.at[:, span], grad.at[0], load_sem.at[5]),
        pltpu.make_async_copy(lat_hbm.at[:, far_span], lat.at[1], load_sem.at[7]),
        pltpu.make_async_copy(grad_hbm.at[:, far_span], grad.at[1], load_sem.at[8]),
        pltpu.make_async_copy(w_hbm, w, load_sem.at[6]),
    ]
    for load in loads:
        load.start()
    pl.semaphore_wait(barrier, 2 * (SIDE - 1) + 4)
    lax.fori_loop(1, SIDE, vouch, 0)

    for load in loads[:8]:
        load.wait()
    target = jnp.where(kept[...] > 0, ids[...] * CAP + slot[...], slots)
    gates = gate[...]

    def build(ahead, carry):
        step = lax.rem(y + ahead, SIDE)
        begin = pl.multiple_of(step * 128, 128)
        slot_of = begin + lax.broadcasted_iota(jnp.int32, (128, 128), 0)
        placed = jnp.zeros((128, 128), F32)
        weight = jnp.zeros((128, 128), F32)
        for k in range(ids.shape[0]):
            same = target[k : k + 1, :] == slot_of
            placed = jnp.where(same, 1.0, placed)
            weight = jnp.where(same, gates[k : k + 1, :], weight)
        hi = weight.astype(BF16)
        here = pl.ds(begin, 128)
        mask[here, :] = placed.astype(BF16)
        gate_hi[here, :] = hi
        gate_lo[here, :] = (weight - hi.astype(F32)).astype(BF16)
        onehot = placed.astype(BF16)
        scale = jnp.sum(weight, axis=1, keepdims=True)
        dests = pl.ds(pl.multiple_of(step * 8, 8), 8)
        for far in range(2):
            lat_rows = contract(onehot, lat[far], 1, 0).astype(BF16)
            grad_rows = (scale * contract(onehot, grad[far], 1, 0)).astype(BF16)
            first = 2 * 16 * far
            outgoing[dests, first : first + 16, :] = lat_rows.reshape(8, 16, SLICE)
            outgoing[dests, first + 16 : first + 32, :] = grad_rows.reshape(8, 16, SLICE)
        return carry

    spans = (pl.ds(0, 32), pl.ds(32, 32))

    def dispatch_row(index, far):
        row = lax.rem(y + STEPS_Y[index], SIDE) * SIDE

        def send(step, carry):
            dest = row + lax.rem(x + step, SIDE)
            pltpu.make_async_remote_copy(
                src_ref=outgoing.at[dest, spans[far]], dst_ref=incoming.at[index * SIDE + step, spans[far]],
                send_sem=out_send.at[far], recv_sem=out_recv.at[far, index // 2],
                device_id={"expert": dest}, device_id_type=MESH,
            ).start()
            return carry

        lax.fori_loop(1 if index == 0 else 0, SIDE, send, 0)

    def dispatch(part, far):
        dispatch_row(2 * part, far)
        dispatch_row(2 * part + 1, far)

    def wait_bytes(ref, sem):
        pltpu.make_async_copy(ref, ref, sem).wait()

    def hop(part, way, kind):
        to, ahead = (above, 1) if way == 0 else (below, RING - 1)
        owner = lax.rem(z + (0, RING - ahead, RING // 2)[kind], RING)
        return pltpu.make_async_remote_copy(
            src_ref=rows.at[part, owner], dst_ref=rows.at[part, owner],
            send_sem=gather_send.at[part, way, kind], recv_sem=gather_recv.at[part, way, kind],
            device_id={"tensor": to}, device_id_type=MESH,
        )

    def landed(part, way, kind):
        behind = RING - 1 if way == 0 else 1
        owner = lax.rem(z + behind + (0, behind, RING // 2)[kind], RING)
        wait_bytes(rows.at[part, owner], gather_recv.at[part, way, kind])

    def unpack(part, far):
        first = part * 2 * SIDE
        if part == 0:
            incoming[0, spans[far]] = outgoing[chip, spans[far]]
            wait_bytes(incoming.at[pl.ds(1, 2 * SIDE - 1), spans[far]], out_recv.at[far, part])
        else:
            wait_bytes(incoming.at[pl.ds(first, 2 * SIDE), spans[far]], out_recv.at[far, part])
        got = incoming[pl.ds(first, 2 * SIDE), spans[far], :].astype(F32).reshape(2 * SIDE, 4, CAP, SLICE)
        for kind in range(2):
            for local in range(LOCAL):
                rows[part, across if far else z, kind, local] = (
                    got[:, 2 * kind + local].reshape(ROWS, SLICE).astype(BF16)
                )

    def enter(part, far):
        unpack(part, far)
        for way in range(2):
            hop(part, way, 2 if far else 0).start()

    def forward(part):
        for way in range(2):
            landed(part, way, 0)
            hop(part, way, 1).start()

    def experts(part):
        for way in range(2):
            landed(part, way, 1)
            landed(part, way, 2)

        def one(local, carry):
            got_in = jnp.concatenate([rows[part, q, 0, local] for q in range(RING)], axis=1)
            got_grad = jnp.concatenate([rows[part, q, 1, local] for q in range(RING)], axis=1)
            active = jnp.maximum(contract(got_in, w[0, local], 1, 0), 0.0)
            unit = (active * active).astype(BF16)
            unit_grad = (contract(got_grad, w[1, local], 1, 0) * 2.0 * active).astype(BF16)
            here = pl.ds(part * ROWS, ROWS)
            hidden[local, here, :] = unit
            pre_grad[local, here, :] = unit_grad
            for q in range(0, RING, 2):
                cols = pl.ds(q * SLICE, 2 * SLICE)
                out_cols = contract(unit, w[1, local, cols, :], 1, 1).astype(BF16)
                in_cols = contract(unit_grad, w[0, local, cols, :], 1, 1).astype(BF16)
                for side in range(2):
                    span = slice(side * SLICE, (side + 1) * SLICE)
                    partial[part, q + side, 0, local] = out_cols[:, span]
                    partial[part, q + side, 1, local] = in_cols[:, span]
            return carry

        lax.fori_loop(0, LOCAL, one, 0)

    def sum_hop(part, way, kind):
        to, ahead = (above, 1) if way == 0 else (below, RING - 1)
        owner = lax.rem(z + ahead * (2, 1, RING // 2 + 1)[kind], RING)
        return owner, pltpu.make_async_remote_copy(
            src_ref=partial.at[part, owner], dst_ref=sums.at[part, way, kind],
            send_sem=sum_send.at[part, way, kind], recv_sem=sum_recv.at[part, way, kind],
            device_id={"tensor": to}, device_id_type=MESH,
        )

    def start_sums(part):
        for kind in (0, 2):
            for way in range(2):
                sum_hop(part, way, kind)[1].start()

    def add(part):
        for way in range(2):
            owner, copy = sum_hop(part, way, 1)
            wait_bytes(sums.at[part, way, 0], sum_recv.at[part, way, 0])
            for kind in range(2):
                for local in range(LOCAL):
                    partial[part, owner, kind, local] = (
                        partial[part, owner, kind, local].astype(F32)
                        + sums[part, way, 0, kind, local].astype(F32)
                    ).astype(BF16)
            copy.start()

    def give_back(part, far):
        pieces = []
        last = 2 if far else 1
        for way in range(2):
            wait_bytes(sums.at[part, way, last], sum_recv.at[part, way, last])
        for kind in range(2):
            for local in range(LOCAL):
                total = partial[part, across if far else z, kind, local].astype(F32)
                for way in range(2):
                    total += sums[part, way, last, kind, local].astype(F32)
                pieces.append(total.reshape(2 * SIDE, CAP, SLICE))
        back[far, pl.ds(part * 2 * SIDE, 2 * SIDE)] = jnp.concatenate(pieces, axis=1).astype(BF16)
        for half in range(2):
            index = 2 * part + half
            row = lax.rem(y + SIDE - STEPS_Y[index], SIDE) * SIDE

            def send(step, carry):
                dest = row + lax.rem(x + SIDE - step, SIDE)
                pltpu.make_async_remote_copy(
                    src_ref=back.at[far, index * SIDE + step], dst_ref=returned.at[far, chip],
                    send_sem=back_send.at[far], recv_sem=back_recv.at[far, part],
                    device_id={"expert": dest}, device_id_type=MESH,
                ).start()
                return carry

            lax.fori_loop(1 if index == 0 else 0, SIDE, send, 0)

    def combine(far):
        out = jnp.zeros((gate_hi.shape[1], SLICE), F32)
        in_grad = jnp.zeros((gate_hi.shape[1], SLICE), F32)
        returned[far, chip] = back[far, 0]
        for index in range(SIDE):
            if index % 2 == 0:
                wait_bytes(returned.at[far, pl.ds(0, 2 * SIDE - (index == 0))], back_recv.at[far, index // 2])
            row = lax.rem(y + STEPS_Y[index], SIDE)
            got = returned[far, pl.ds(row * SIDE, SIDE)]
            out_rows = got[:, 0:16].reshape(SIDE * 16, SLICE)
            in_rows = got[:, 16:32].reshape(SIDE * 16, SLICE)
            here = pl.ds(pl.multiple_of(row * SIDE * 16, SIDE * 16), SIDE * 16)
            out += contract(gate_hi[here, :], out_rows, 0, 0) + contract(gate_lo[here, :], out_rows, 0, 0)
            in_grad += contract(mask[here, :], in_rows, 0, 0)
        return out, in_grad

    def terms(kind, mine):
        half = dp if mine else 1 - dp
        store = keep_half if mine else send_half
        other = pre_grad if kind == 0 else hidden

        def one(step, carry):
            local, q = lax.div(step, RING // 2), lax.rem(step, RING // 2)
            left = jnp.concatenate(
                [rows[part, half * (RING // 2) + q, kind, local] for part in range(PARTS)], axis=0
            )
            span = pl.ds(pl.multiple_of(q * SLICE, SLICE), SLICE)
            store[kind, local, span, :] = contract(left, other[local], 0, 0).astype(BF16)
            return carry

        lax.fori_loop(0, LOCAL * (RING // 2), one, 0)

    term_copy = pltpu.make_async_remote_copy(
        src_ref=send_half, dst_ref=got_terms, send_sem=term_send, recv_sem=term_recv,
        device_id={"dp": 1 - dp}, device_id_type=MESH,
    )
    keep_copy = pltpu.make_async_copy(keep_half, own_terms, keep_sem)

    far_copy = pltpu.make_async_remote_copy(
        src_ref=far_send, dst_ref=far_got, send_sem=far_sems.at[0], recv_sem=far_sems.at[1],
        device_id={"tensor": across}, device_id_type=MESH,
    )

    build(STEPS_Y[0], 0)
    dispatch_row(0, 0)
    build(STEPS_Y[1], 0)
    pl.semaphore_wait(row_here, SIDE - 1)
    dispatch_row(1, 0)
    lax.fori_loop(1, 4, build, 0)
    lax.fori_loop(5, SIDE, build, 0)
    dispatch(1, 0)
    enter(0, 0)
    dispatch(2, 0)
    enter(1, 0)
    dispatch(3, 0)
    enter(2, 0)
    dispatch(0, 1)
    enter(3, 0)
    dispatch(1, 1)
    forward(0)
    dispatch(2, 1)
    forward(1)
    dispatch(3, 1)
    forward(2)
    forward(3)
    for part in range(PARTS):
        enter(part, 1)
    loads[8].wait()
    for part in range(PARTS):
        experts(part)
        start_sums(part)
    for part in range(PARTS):
        add(part)
        give_back(part, 1)
    terms(0, False)
    terms(1, False)
    term_copy.start()
    give_back(0, 0)
    terms(0, True)
    give_back(1, 0)
    terms(1, True)
    keep_copy.start()
    far_out, far_in = combine(1)
    far_send[0] = far_out.astype(BF16)
    far_send[1] = far_in.astype(BF16)
    give_back(2, 0)
    give_back(3, 0)
    far_copy.start()
    out, in_grad = combine(0)
    far_copy.wait_recv()
    mixed[...] = (out + far_got[0].astype(F32)).astype(BF16)
    lat_grad[...] = (in_grad + far_got[1].astype(F32)).astype(BF16)

    term_copy.wait()
    keep_copy.wait()
    far_copy.wait_send()
    for far in range(2):
        wait_bytes(outgoing.at[pl.ds(0, peers - 1), spans[far]], out_send.at[far])
        wait_bytes(back.at[far, pl.ds(0, peers - 1)], back_send.at[far])
    for part in range(PARTS):
        for way in range(2):
            for kind in range(STEPS):
                hop(part, way, kind).wait_send()
                sum_hop(part, way, kind)[1].wait_send()


def shards(latent, grad_out, expert_weights, expert_ids, slot_index, kept, gate_weights):
    tokens, width = latent.shape
    units = expert_weights.shape[3]
    topk = expert_ids.shape[1]
    peers = lax.axis_size("expert")
    slots = peers * LOCAL * CAP
    half = width // 2
    vmem = pl.BlockSpec(memory_space=pltpu.VMEM)
    anywhere = pl.BlockSpec(memory_space=pl.ANY)
    hbm = pl.BlockSpec(memory_space=pltpu.HBM)
    dma = pltpu.SemaphoreType.DMA
    ring = (PARTS, 2, STEPS)
    mixed, lat_grad, own, got = pl.pallas_call(
        block_kernel,
        out_shape=(
            jax.ShapeDtypeStruct((tokens, SLICE), BF16),
            jax.ShapeDtypeStruct((tokens, SLICE), BF16),
            jax.ShapeDtypeStruct((2, LOCAL, half, units), BF16),
            jax.ShapeDtypeStruct((2, LOCAL, half, units), BF16),
        ),
        in_specs=[hbm] * 7,
        out_specs=(vmem, vmem, anywhere, anywhere),
        scratch_shapes=[
            pltpu.VMEM((topk, tokens), jnp.int32),
            pltpu.VMEM((topk, tokens), jnp.int32),
            pltpu.VMEM((topk, tokens), jnp.int32),
            pltpu.VMEM((topk, tokens), F32),
            pltpu.VMEM((2, tokens, SLICE), BF16),
            pltpu.VMEM((2, tokens, SLICE), BF16),
            pltpu.VMEM((2, LOCAL, width, units), BF16),
            pltpu.VMEM((slots, tokens), BF16),
            pltpu.VMEM((slots, tokens), BF16),
            pltpu.VMEM((slots, tokens), BF16),
            pltpu.VMEM((peers, 64, SLICE), BF16),
            pltpu.VMEM((peers, 64, SLICE), BF16),
            pltpu.VMEM((PARTS, RING, 2, LOCAL, ROWS, SLICE), BF16),
            pltpu.VMEM((PARTS, RING, 2, LOCAL, ROWS, SLICE), BF16),
            pltpu.VMEM(ring + (2, LOCAL, ROWS, SLICE), BF16),
            pltpu.VMEM((2, peers, 32, SLICE), BF16),
            pltpu.VMEM((2, peers, 32, SLICE), BF16),
            pltpu.VMEM((2, tokens, SLICE), BF16),
            pltpu.VMEM((2, tokens, SLICE), BF16),
            pltpu.VMEM((LOCAL, PARTS * ROWS, units), BF16),
            pltpu.VMEM((LOCAL, PARTS * ROWS, units), BF16),
            pltpu.VMEM((2, LOCAL, half, units), BF16),
            pltpu.VMEM((2, LOCAL, half, units), BF16),
            dma((9,)),
            dma((2,)),
            dma((2, PARTS)),
            dma(ring),
            dma(ring),
            dma(ring),
            dma(ring),
            dma((2,)),
            dma((2, PARTS)),
            dma((2,)),
            dma,
            dma,
            dma,
            pltpu.SemaphoreType.REGULAR,
        ],
        compiler_params=pltpu.CompilerParams(
            collective_id=0, has_side_effects=True, vmem_limit_bytes=60 * 2**20
        ),
    )(expert_ids.T, slot_index.T, kept.T, gate_weights.T, latent, grad_out, expert_weights)
    return (mixed, lat_grad, own.astype(F32) + got.astype(F32))


def solution(mesh):
    in_specs = (
        P(("dp", "expert"), None),
        P(("dp", "expert"), None),
        P(None, "expert", None, "tensor"),
        P(("dp", "expert"), None),
        P(("dp", "expert"), None),
        P(("dp", "expert"), None),
        P(("dp", "expert"), None),
    )
    out_specs = (
        P(("dp", "expert"), "tensor"),
        P(("dp", "expert"), "tensor"),
        P(None, "expert", "dp", "tensor"),
    )
    return jax.shard_map(shards, mesh=mesh, in_specs=in_specs, out_specs=out_specs, check_vma=False)
```

time: 137 us -> 121 us (0.88)
  the two profiles are of different devices: /device:TPU:2 before, /device:TPU:16 now
where the time goes in v2:
time: 121 us
  Pallas kernels  116 us (96%)
  other arithmetic  3.1 us (3%)
  local copies, waits for them, and re-layouts  1.24 us (1%)
    pallas_call x1, Pallas kernels, shards(): pl.pallas_call(block_kernel, out_shape=(jax.ShapeDtypeStruct((tokens, SLI...  116 us
    add x1, other arithmetic, shards(): return (mixed, lat_grad, own.astype(F32) + got.astype(F32))  3.1 us

profile of v2, /device:TPU:16, one launch (start us, length us, event | category | flops | bytes accessed | tf_op | source)
XLA Modules:
  0.0 121.0 jit_solution(570459027753748054)
XLA Ops:
  0.6 116.0 %shard_map.94 = (bf16[128,128]{1,0:T(8,128)(2,1)}, bf16[128,128]{1,0:T(8,128)(2,1)}, bf16[2,2,512,256]{3,2,1,0:T(8,128)(2,1)}, bf16[2,2,512,256]{3,2,1,0:T(8,128)(2,1)}) custom-call(s32[8,128]{1,0:T(8,128)} %bitcast.4, s32[8,128]{1,0:T(8,128)} %bitcast.5, s32[8,128]{1,0:T(8,128)} %bitcast.6, f32[8,128]{1,0:T(8,128)} %bitcast.7, bf16[128,1024]{1,0:T(8,128)(2,1)} %lat_hbm.1, ...), custom_call_target="tpu_custom_call" | custom-call | tf_op jit(solution)/shard_map/pallas_call | solution.py:374
  116.6 0.0 copy-start.1
  116.6 0.0 copy-start
  116.7 3.1 %convert_add_fusion = f32[2,2,512,256]{3,2,1,0:T(8,128)} fusion(bf16[2,2,512,256]{3,2,1,0:T(8,128)(2,1)} %get-tuple-element.10, bf16[2,2,512,256]{3,2,1,0:T(8,128)(2,1)} %get-tuple-element.9), kind=kLoop, calls=%fused_computation | loop fusion | flops 1572864 | bytes 4194304 | tf_op jit(solution)/shard_map/add | solution.py:427
  119.8 0.0 copy-done.1
  119.8 0.6 copy.12
  120.4 0.0 copy-done
  120.4 0.6 copy.13
Async XLA Ops:
  116.6 3.1 %copy-start.1 = (bf16[128,128]{1,0:T(8,128)(2,1)S(1)}, bf16[128,128]{1,0:T(8,128)(2,1)}, u32[]{:S(2)}) copy-start(bf16[128,128]{1,0:T(8,128)(2,1)} %get-tuple-element.14) | copy-start | bytes 98308
  116.6 3.7 %copy-start = (bf16[128,128]{1,0:T(8,128)(2,1)S(1)}, bf16[128,128]{1,0:T(8,128)(2,1)}, u32[]{:S(2)}) copy-start(bf16[128,128]{1,0:T(8,128)(2,1)} %get-tuple-element.15) | copy-start | bytes 98308
